TPU v7x, 32 devices: a whole 2x2x4 slice. The times are simulated.
32 devices in a mesh: groups: 2 (over y), graph: 2 (over x), feat: 4 (over z), sub: 2 (over core).
Axes of the slice: x: 2, y: 2, z: 4, core: 2. Of those that a mesh axis runs over, the one named last changes fastest.
Arguments:
- node_features: bfloat16 [12288, 128], P(('groups', 'graph', 'feat', 'sub')), parts along dimension 0, may hold values from -6 to 6
- edge_features: bfloat16 [131072, 128], P(('groups', 'graph', 'feat', 'sub')), parts along dimension 0, may hold values from -6 to 6
- node_cotangent: bfloat16 [12288, 128], P(('groups', 'graph', 'feat', 'sub')), parts along dimension 0, may hold values from -6 to 6
- edge_cotangent: bfloat16 [131072, 128], P(('groups', 'graph', 'feat', 'sub')), parts along dimension 0, may hold values from -6 to 6
- senders: int32 [131072], P(('groups', 'graph', 'feat', 'sub')), parts along dimension 0, may hold values from 0 to 3199, as said below
- receivers: int32 [131072], P(('groups', 'graph', 'feat', 'sub')), parts along dimension 0, may hold values from 0 to 383
- send_rows: int32 [4, 2, 64], P(('groups', 'graph')), parts along dimension 0, may hold values from 0 to 3071
- live_edges: int32 [32], P(('groups', 'graph', 'feat', 'sub')), parts along dimension 0, may hold values from 1024 to 4096, as said below
- edge_in_weight: bfloat16 [384, 128], replicated, may hold values from -0.3125 to 0.3125
- edge_out_weight: bfloat16 [128, 128], replicated, may hold values from -0.5 to 0.5
- edge_bias: float32 [128], replicated, may hold values from -3 to 3
- edge_gain: float32 [128], replicated, may hold values from 0.25 to 1.75
- edge_shift: float32 [128], replicated, may hold values from -3 to 3
- node_in_weight: bfloat16 [256, 128], replicated, may hold values from -0.375 to 0.375
- node_out_weight: bfloat16 [128, 128], replicated, may hold values from -0.5 to 0.5
- node_bias: float32 [128], replicated, may hold values from -3 to 3
- node_gain: float32 [128], replicated, may hold values from 0.25 to 1.75
Outputs:
- node_grads: float32 [12288, 128], P(('groups', 'graph', 'feat', 'sub')), parts along dimension 0
- edge_grads: float32 [131072, 128], P(('groups', 'graph', 'feat', 'sub')), parts along dimension 0
- edge_in_grad: float32 [768, 128], P('groups'), parts along dimension 0
- edge_out_grad: float32 [256, 128], P('groups'), parts along dimension 0
- node_in_grad: float32 [512, 128], P('groups'), parts along dimension 0
- node_out_grad: float32 [256, 128], P('groups'), parts along dimension 0
- vector_grads: float32 [12, 128], P('groups'), parts along dimension 0
There are 2 independent parts, one for each index of `groups`. A program takes and returns all parts, laid end to end along the dimension named above; an argument that names none is the same for every part. Nothing has to cross between parts.
Inputs may be any that keep to these rules, and one draw needn't show every extreme that they name: A sender below 3072 is a row of the edge's own partition; 3072 + q * 64 + k names the k-th row that partition q sends to it. Most senders lie among the rows of the edge's own device and the two slices beside it within the partition. `receivers`: a row of the edge's own device's nodes. send_rows[p, q, k] is the row of partition p's nodes that it sends to partition q as its k-th boundary row; rows may repeat. Slots from live_edges[d] on are padding; some device's slots are all used.
All inputs are finite; a program needn't handle non-finite values.
Results may differ from a plain program's by a relative error of at most 0.0066.
Values may be sent and summed in bfloat16 or wider, within the bound.
A program may use at most 128 MiB of HBM per device.

v0:
```python
import jax
import jax.numpy as jnp
from jax import lax
from jax.sharding import PartitionSpec as P

epsilon = 1e-05


def norm_forward(output, gains, shifts):
    average = jnp.mean(output, axis=-1, keepdims=True)
    centred = output - average
    inverse = lax.rsqrt(jnp.mean(centred * centred, axis=-1, keepdims=True) + epsilon)
    normed = centred * inverse
    return (normed * gains + shifts, normed, inverse)


def mlp_forward(inputs, w_in, biases, w_out, gains, shifts):
    preact = jnp.dot(inputs, w_in, preferred_element_type=jnp.float32) + biases
    hidden = (preact * jax.nn.sigmoid(preact)).astype(jnp.bfloat16)
    output = jnp.dot(hidden, w_out, preferred_element_type=jnp.float32)
    result, normed, inverse = norm_forward(output, gains, shifts)
    return (result, (preact, hidden, normed, inverse))


def mlp_backward(d_result, inputs, w_in, w_out, gains, stored):
    preact, hidden, normed, inverse = stored
    d_normed = d_result * gains
    d_output = inverse * (
        d_normed
        - jnp.mean(d_normed, axis=-1, keepdims=True)
        - normed * jnp.mean(d_normed * normed, axis=-1, keepdims=True)
    )
    d_output_b = d_output.astype(jnp.bfloat16)
    grad_out = lax.dot_general(
        hidden, d_output_b, (((0,), (0,)), ((), ())), preferred_element_type=jnp.float32
    )
    d_hidden = lax.dot_general(
        d_output_b, w_out, (((1,), (1,)), ((), ())), preferred_element_type=jnp.float32
    )
    sigmoid = jax.nn.sigmoid(preact)
    d_preact = d_hidden * sigmoid * (1.0 + preact * (1.0 - sigmoid))
    d_preact_b = d_preact.astype(jnp.bfloat16)
    grad_in = lax.dot_general(
        inputs, d_preact_b, (((0,), (0,)), ((), ())), preferred_element_type=jnp.float32
    )
    d_inputs = lax.dot_general(
        d_preact_b, w_in, (((1,), (1,)), ((), ())), preferred_element_type=jnp.float32
    )
    vectors = jnp.stack(
        [jnp.sum(d_preact, axis=0), jnp.sum(d_result * normed, axis=0), jnp.sum(d_result, axis=0)]
    )
    return (d_inputs, grad_in, grad_out, vectors)


def local_layer(
    lookup, node_rows, node_cot, edge_rows, edge_cot, sender_ids, receiver_ids, live_count, params
):
    (
        edge_in_weight,
        edge_out_weight,
        edge_bias,
        edge_gain,
        edge_shift,
        node_in_weight,
        node_out_weight,
        node_bias,
        node_gain,
    ) = params
    edge_count = edge_rows.shape[0]
    node_count = node_rows.shape[0]
    width = node_rows.shape[1]
    live_mask = (jnp.arange(edge_count, dtype=jnp.int32) < live_count).astype(jnp.float32)[:, None]
    edge_inputs = jnp.concatenate([edge_rows, lookup[sender_ids], node_rows[receiver_ids]], axis=1)
    edge_update, edge_stored = mlp_forward(
        edge_inputs, edge_in_weight, edge_bias, edge_out_weight, edge_gain, edge_shift
    )
    edge_new = edge_rows.astype(jnp.float32) + live_mask * edge_update
    gathered = jax.ops.segment_sum(live_mask * edge_new, receiver_ids, num_segments=node_count)
    node_inputs = jnp.concatenate([node_rows, gathered.astype(jnp.bfloat16)], axis=1)
    node_update, node_stored = mlp_forward(
        node_inputs,
        node_in_weight,
        node_bias,
        node_out_weight,
        node_gain,
        jnp.zeros_like(node_gain),
    )
    node_delta = node_cot.astype(jnp.float32)
    d_node_inputs, grad_node_in, grad_node_out, node_vectors = mlp_backward(
        node_delta, node_inputs, node_in_weight, node_out_weight, node_gain, node_stored
    )
    d_gathered = d_node_inputs[:, width:]
    d_edge_total = edge_cot.astype(jnp.float32) + live_mask * d_gathered[receiver_ids]
    d_edge_inputs, grad_edge_in, grad_edge_out, edge_vectors = mlp_backward(
        live_mask * d_edge_total,
        edge_inputs,
        edge_in_weight,
        edge_out_weight,
        edge_gain,
        edge_stored,
    )
    edge_grads = d_edge_total + d_edge_inputs[:, :width]
    d_lookup = jax.ops.segment_sum(
        d_edge_inputs[:, width : 2 * width], sender_ids, num_segments=lookup.shape[0]
    )
    node_grads = (
        node_delta
        + d_node_inputs[:, :width]
        + jax.ops.segment_sum(d_edge_inputs[:, 2 * width :], receiver_ids, num_segments=node_count)
    )
    terms = (
        grad_edge_in,
        grad_edge_out,
        grad_node_in,
        grad_node_out,
        jnp.concatenate([edge_vectors, node_vectors], axis=0),
    )
    return (node_grads, edge_grads, d_lookup, terms)


def per_device(
    node_features,
    edge_features,
    node_cotangent,
    edge_cotangent,
    senders,
    receivers,
    send_rows,
    live_edges,
    edge_in_weight,
    edge_out_weight,
    edge_bias,
    edge_gain,
    edge_shift,
    node_in_weight,
    node_out_weight,
    node_bias,
    node_gain,
):
    params = (
        edge_in_weight,
        edge_out_weight,
        edge_bias,
        edge_gain,
        edge_shift,
        node_in_weight,
        node_out_weight,
        node_bias,
        node_gain,
    )
    slices = lax.axis_size(("feat", "sub"))
    partition = lax.all_gather(node_features, ("feat", "sub"), axis=0, tiled=True)
    node_part = partition.shape[0]
    width = partition.shape[1]
    row_lists = send_rows[0]
    peer_count = row_lists.shape[0]
    per_peer = row_lists.shape[1]
    outgoing = partition[row_lists]
    arrived = lax.all_to_all(outgoing, "graph", split_axis=0, concat_axis=0, tiled=True)
    lookup = jnp.concatenate([partition, arrived.reshape(peer_count * per_peer, width)], axis=0)
    node_grads, edge_grads, d_lookup, terms = local_layer(
        lookup,
        node_features,
        node_cotangent,
        edge_features,
        edge_cotangent,
        senders,
        receivers,
        live_edges[0],
        params,
    )
    grad_edge_in, grad_edge_out, grad_node_in, grad_node_out, vector_terms = terms
    summed = lax.psum(
        (grad_edge_in, grad_edge_out, grad_node_in, grad_node_out, vector_terms),
        ("graph", "feat", "sub"),
    )
    d_boundary = d_lookup[node_part:].reshape(peer_count, per_peer, width)
    partial_value = d_lookup[:node_part]
    returned = lax.all_to_all(
        d_boundary.astype(jnp.bfloat16), "graph", split_axis=0, concat_axis=0, tiled=True
    ).astype(d_boundary.dtype)
    partial_value = partial_value + jax.ops.segment_sum(
        returned.reshape(-1, width), row_lists.reshape(-1), num_segments=node_part
    )
    node_total = node_grads + lax.psum_scatter(
        partial_value.astype(jnp.bfloat16), ("feat", "sub"), scatter_dimension=0, tiled=True
    ).astype(jnp.float32)
    device_count = lax.axis_size("graph") * slices
    edge_scale = float(device_count * edge_features.shape[0]) ** (-0.5)
    node_scale = float(device_count * node_features.shape[0]) ** (-0.5)
    row_scales = jnp.array([edge_scale] * 3 + [node_scale] * 3, jnp.float32)[:, None]
    return (
        node_total,
        edge_grads,
        summed[0] * edge_scale,
        summed[1] * edge_scale,
        summed[2] * node_scale,
        summed[3] * node_scale,
        summed[4] * row_scales,
    )


def solution(mesh):
    in_specs = (
        P(("groups", "graph", "feat", "sub"), None),
        P(("groups", "graph", "feat", "sub"), None),
        P(("groups", "graph", "feat", "sub"), None),
        P(("groups", "graph", "feat", "sub"), None),
        P(("groups", "graph", "feat", "sub")),
        P(("groups", "graph", "feat", "sub")),
        P(("groups", "graph"), None, None),
        P(("groups", "graph", "feat", "sub")),
        P(),
        P(),
        P(),
        P(),
        P(),
        P(),
        P(),
        P(),
        P(),
    )
    out_specs = (
        P(("groups", "graph", "feat", "sub"), None),
        P(("groups", "graph", "feat", "sub"), None),
        P("groups", None),
        P("groups", None),
        P("groups", None),
        P("groups", None),
        P("groups", None),
    )
    return jax.shard_map(
        per_device, mesh=mesh, in_specs=in_specs, out_specs=out_specs, check_vma=False
    )
```

profile of v0, /device:TPU:0, one launch (start us, length us, event | category | flops | bytes accessed | tf_op | source)
XLA Modules:
  0.0 270.4 jit_solution(11376892056609187474)
XLA Ops:
  8.0 17.6 %all_gather.3 = bf16[3072,128]{1,0:T(8,128)(2,1)S(1)} all-gather(bf16[384,128]{1,0:T(8,128)(2,1)} %param.18), channel_id=1, replica_groups=mesh['groups'=2,'graph'=2,'feat'=4,'sub'=2] {'feat','sub'}, dimensions={0}, use_global_device_ids=true | all-gather | bytes 884736 | tf_op jit(solution)/shard_map/all_gather | solution.py:152
  27.7 3.3 %all-to-all-start = ((bf16[2,64,128]{2,1,0:T(8,128)(2,1)}), bf16[2,64,128]{2,1,0:T(8,128)(2,1)S(1)}, u32[]{:S(2)}, u32[]{:S(2)}) async-start(bf16[2,64,128]{2,1,0:T(8,128)(2,1)} %bitcast.2), calls=%async_computation | async-start | bytes 65536 | tf_op jit(solution)/shard_map/all_to_all | solution.py:159
  31.7 2.4 constant_dynamic-update-slice_fusion.2
  36.7 12.1 %gather_fusion.2 = bf16[4096,128]{1,0:T(8,128)(2,1)S(1)} fusion(bf16[384,128]{1,0:T(8,128)(2,1)S(1)} %copy-done.1, s32[4096]{0:T(1024)S(1)} %fusion.29), kind=kCustom, calls=%fused_computation.2 | custom fusion | bytes 2113536 | tf_op jit(solution)/shard_map/gather | solution.py:73
  49.6 2.3 copy.49
  52.0 15.0 %gather_fusion.1 = bf16[4096,128]{1,0:T(8,128)(2,1)} fusion(bf16[3200,128]{1,0:T(8,128)(2,1)S(1)} %pad_maximum_fusion, s32[4096]{0:T(1024)S(1)} %fusion.28), kind=kCustom, calls=%fused_computation.1 | custom fusion | bytes 2113536 | tf_op jit(solution)/shard_map/gather | solution.py:73
  67.0 2.3 constant_dynamic-update-slice_fusion.1
  70.5 4.3 %multiply_convert_fusion.1 = (bf16[4096,128]{1,0:T(8,128)(2,1)S(1)}, f32[4096,128]{1,0:T(8,128)}) fusion(f32[128]{0:T(128)S(1)} %copy-done.32, bf16[4096,384]{1,0:T(8,128)(2,1)} %constant_dynamic-update-slice_fusion, bf16[384,128]{1,0:T(8,128)(2,1)S(1)} %copy-done), kind=kOutput, calls=%fused_computation.21 | convolution fusion | flops 405798912 | bytes 6390272 | tf_op jit(solution)/shard_map/dot_general | solution.py:18
  76.0 2.0 add_multiply_fusion
  78.0 2.9 %copy.47 = f32[4096,128]{1,0:T(8,128)} copy(f32[4096,128]{0,1:T(8,128)} %add_multiply_fusion) | data formatting | bytes 4194304 | tf_op jit(solution)/shard_map/mul | solution.py:78
  81.0 22.9 %scatter_custom_fusion = f32[384,128]{1,0:T(8,128)S(1)} fusion(s32[4096]{0:T(1024)} %param.23, f32[4096,128]{1,0:T(8,128)} %copy.47, f32[]{:T(128)} %constant.11.clone.1), kind=kCustom, calls=%fused_computation.55 | custom fusion | flops 524288 | bytes 197120 | tf_op jit(solution)/shard_map/scatter-add | solution.py:78
  110.4 15.4 %gather_fusion.3 = f32[4096,128]{1,0:T(8,128)} fusion(f32[384,128]{1,0:T(8,128)S(1)} %get-tuple-element.41, s32[4096]{0:T(1024)} %copy-done.14), kind=kCustom, calls=%fused_computation.3 | custom fusion | bytes 4210688 | tf_op jit(solution)/shard_map/gather | solution.py:93
  125.8 3.0 %copy.50 = f32[4096,128]{0,1:T(8,128)} copy(f32[4096,128]{1,0:T(8,128)} %gather_fusion.3) | data formatting | bytes 4194304 | tf_op jit(solution)/shard_map/gather | solution.py:93
  128.8 3.7 %multiply_reduce_fusion = (f32[128]{0:T(128)}, f32[4096]{0:T(1024)S(1)}, f32[4096]{0:T(1024)S(1)}, f32[128]{0:T(128)}, f32[4096,128]{0,1:T(8,128)S(1)}) fusion(f32[4096,128]{0,1:T(8,128)S(1)} %get-tuple-element.46, f32[4096]{0:T(1024)S(1)} %copy-done.12, f32[4096]{0:T(1024)S(1)} %broadcast_multiply_fusion.6, f32[4096]{0:T(1024)S(1)} %copy-done.10, ...), kind=kLoop, calls=%fused_computation.15 | loop fusion | flops 6807296 | bytes 7423488 | tf_op jit(solution)/shard_map/reduce_sum | solution.py:50
  139.0 3.6 %fusion.9 = f32[4096,384]{1,0:T(8,128)} fusion(bf16[384,128]{1,0:T(8,128)(2,1)S(1)} %copy-done, bf16[4096,128]{1,0:T(8,128)(2,1)S(1)} %get-tuple-element.52), kind=kOutput, calls=%fused_computation.33 | convolution fusion | flops 402653184 | bytes 7438336 | tf_op jit(solution)/shard_map/dot_general | solution.py:46
  142.7 21.1 %scatter_custom_fusion.1 = f32[3200,128]{1,0:T(8,128)S(1)} fusion(s32[4096]{0:T(1024)} %param.22, f32[4096,384]{1,0:T(8,128)} %fusion.9, f32[]{:T(128)} %constant.11.clone.1), kind=kCustom, calls=%fused_computation.13 | custom fusion | flops 524288 | bytes 3736064 | tf_op jit(solution)/shard_map/scatter-add | solution.py:103
  164.4 3.3 %all-to-all-start.1 = ((bf16[2,64,128]{2,1,0:T(8,128)(2,1)}), bf16[2,64,128]{2,1,0:T(8,128)(2,1)S(1)}, u32[]{:S(2)}, u32[]{:S(2)}) async-start(bf16[2,64,128]{2,1,0:T(8,128)(2,1)} %bitcast.4), calls=%async_computation.1 | async-start | bytes 65536 | tf_op jit(solution)/shard_map/all_to_all | solution.py:179
  167.9 3.7 %all-to-all-done.1 = bf16[2,64,128]{2,1,0:T(8,128)(2,1)S(1)} async-done(((bf16[2,64,128]{2,1,0:T(8,128)(2,1)}), bf16[2,64,128]{2,1,0:T(8,128)(2,1)S(1)}, u32[]{:S(2)}, u32[]{:S(2)}) %all-to-all-start.1) | async-done | bytes 32800 | tf_op jit(solution)/shard_map/all_to_all | solution.py:179
  171.6 1.8 scatter_custom_fusion.2
  177.9 2.5 add.146
  180.4 1.8 copy.54
  182.4 31.8 %psum.39 = f32[6,128]{1,0:T(8,128)S(1)} all-reduce(f32[6,128]{1,0:T(8,128)S(1)} %concatenate.15), channel_id=1, replica_groups=mesh['groups'=2,'graph'=2,'feat'=4,'sub'=2] {'graph','feat','sub'}, use_global_device_ids=true, to_apply=%region_23.0 | all-reduce | flops 768 | bytes 6144 | tf_op jit(solution)/shard_map/psum | solution.py:173
  214.9 17.1 %all-reduce.3.cloned.1.call-done = (f32[384,128]{1,0:T(8,128)}, f32[128,128]{1,0:T(8,128)}, f32[256,128]{1,0:T(8,128)}, f32[128,128]{1,0:T(8,128)}) async-done(((f32[384,128]{1,0:T(8,128)}, f32[128,128]{1,0:T(8,128)}, f32[256,128]{1,0:T(8,128)}, f32[128,128]{1,0:T(8,128)}), (f32[384,128]{1,0:T(8,128)}, f32[128,128]{1,0:T(8,128)}, f32[256,128]{1,0:T(8,128)}, ...) | async-done | bytes 458768 | tf_op jit(solution)/shard_map/psum | solution.py:173
  239.3 22.9 %scatter_custom_fusion.3 = f32[384,128]{1,0:T(8,128)S(1)} fusion(f32[384,128]{1,0:T(8,128)S(1)} %copy.52, s32[4096]{0:T(1024)} %param.23, f32[4096,384]{1,0:T(8,128)} %fusion.9), kind=kCustom, calls=%fused_computation.11 | custom fusion | flops 524288 | bytes 2293760 | tf_op jit(solution)/shard_map/scatter-add | solution.py:109
  (126 shorter events, 35.1 us)
Async XLA Ops:
  8.0 62.5 %copy-start = (bf16[384,128]{1,0:T(8,128)(2,1)S(1)}, bf16[384,128]{1,0:T(8,128)(2,1)}, u32[]{:S(2)}) copy-start(bf16[384,128]{1,0:T(8,128)(2,1)} %param.26) | copy-start | bytes 294916
  8.0 27.4 %copy-start.4 = (bf16[4096,128]{1,0:T(8,128)(2,1)S(1)}, bf16[4096,128]{1,0:T(8,128)(2,1)}, u32[]{:S(2)}) copy-start(bf16[4096,128]{1,0:T(8,128)(2,1)} %param.19) | copy-start | bytes 3145732
  8.0 26.1 %copy-start.20 = (s32[4096]{0:T(1024)S(1)}, s32[4096]{0:T(1024)}, u32[]{:S(2)}) copy-start(s32[4096]{0:T(1024)} %param.23) | copy-start | bytes 49156
  27.7 24.3 %all-to-all-start = ((bf16[2,64,128]{2,1,0:T(8,128)(2,1)}), bf16[2,64,128]{2,1,0:T(8,128)(2,1)S(1)}, u32[]{:S(2)}, u32[]{:S(2)}) async-start(bf16[2,64,128]{2,1,0:T(8,128)(2,1)} %bitcast.2), calls=%async_computation | async-start | bytes 65536 | tf_op jit(solution)/shard_map/all_to_all | solution.py:159
  31.0 201.0 %all-reduce.3.cloned.1.call-start = ((), (), s32[]{:S(2)}) async-start(), calls=%async_computation.4 | async-start | bytes 917504 | tf_op jit(solution)/shard_map/psum | solution.py:173
  31.7 5.0 %copy-start.1 = (bf16[384,128]{1,0:T(8,128)(2,1)S(1)}, bf16[384,128]{1,0:T(8,128)(2,1)}, u32[]{:S(2)}) copy-start(bf16[384,128]{1,0:T(8,128)(2,1)} %param.18) | copy-start | bytes 294916
  34.1 14.7 %copy-start.14 = (s32[4096]{0:T(1024)}, s32[4096]{0:T(1024)S(1)}, u32[]{:S(2)}) copy-start(s32[4096]{0:T(1024)S(1)} %fusion.29) | copy-start | bytes 49156
  36.7 12.1 %copy-start.15 = (bf16[384,128]{1,0:T(8,128)(2,1)S(1)}, bf16[384,128]{1,0:T(8,128)(2,1)}, u32[]{:S(2)}) copy-start(bf16[384,128]{1,0:T(8,128)(2,1)} %param.20) | copy-start | bytes 294916
  67.0 3.5 %copy-start.32 = (f32[128]{0:T(128)S(1)}, f32[128]{0:T(128)}, u32[]{:S(2)}) copy-start(f32[128]{0:T(128)} %param.28) | copy-start | bytes 1540
  70.5 4.3 %copy-start.17 = (bf16[128,128]{1,0:T(8,128)(2,1)S(1)}, bf16[128,128]{1,0:T(8,128)(2,1)}, u32[]{:S(2)}) copy-start(bf16[128,128]{1,0:T(8,128)(2,1)} %param.27) | copy-start | bytes 98308
  103.9 2.3 copy-start.6
  103.9 2.3 copy-start.23
  103.9 3.9 %copy-start.19 = (bf16[128,128]{1,0:T(8,128)(2,1)S(1)}, bf16[128,128]{1,0:T(8,128)(2,1)}, u32[]{:S(2)}) copy-start(bf16[128,128]{1,0:T(8,128)(2,1)} %param.32) | copy-start | bytes 98308
  103.9 4.7 %copy-start.16 = (bf16[256,128]{1,0:T(8,128)(2,1)S(1)}, bf16[256,128]{1,0:T(8,128)(2,1)}, u32[]{:S(2)}) copy-start(bf16[256,128]{1,0:T(8,128)(2,1)} %param.31) | copy-start | bytes 196612
  125.8 3.0 %copy-start.10 = (f32[4096]{0:T(1024)S(1)}, f32[4096]{0:T(1024)}, u32[]{:S(2)}) copy-start(f32[4096]{0:T(1024)} %fusion.30) | copy-start | bytes 49156
  125.8 3.0 %copy-start.12 = (f32[4096]{0:T(1024)S(1)}, f32[4096]{0:T(1024)}, u32[]{:S(2)}) copy-start(f32[4096]{0:T(1024)} %copy-done.11) | copy-start | bytes 49156
  125.8 3.0 %copy-start.22 = (f32[128]{0:T(128)S(1)}, f32[128]{0:T(128)}, u32[]{:S(2)}) copy-start(f32[128]{0:T(128)} %param.29) | copy-start | bytes 1540
  142.7 25.0 %copy-start.28 = (s32[1,2,64]{2,1,0:T(2,128)S(1)}, s32[1,2,64]{2,1,0:T(2,128)}, u32[]{:S(2)}) copy-start(s32[1,2,64]{2,1,0:T(2,128)} %param.24) | copy-start | bytes 1540
  164.4 7.2 %all-to-all-start.1 = ((bf16[2,64,128]{2,1,0:T(8,128)(2,1)}), bf16[2,64,128]{2,1,0:T(8,128)(2,1)S(1)}, u32[]{:S(2)}, u32[]{:S(2)}) async-start(bf16[2,64,128]{2,1,0:T(8,128)(2,1)} %bitcast.4), calls=%async_computation.1 | async-start | bytes 65536 | tf_op jit(solution)/shard_map/all_to_all | solution.py:179
  167.7 70.5 %reduce-scatter.4.cloned.1.call-start = ((), (), s32[]{:S(2)}) async-start(), calls=%async_computation.3 | async-start | bytes 884736
  180.3 2.0 copy-start.24
  180.3 2.0 copy-start.25
  180.4 33.8 %copy-start.31 = (f32[6]{0:T(128)S(1)}, f32[6]{0:T(128)}, u32[]{:S(2)}) copy-start(f32[6]{0:T(128)} %constant.10.clone) | copy-start | bytes 76
  180.4 58.8 %copy-start.7 = (bf16[384,128]{0,1:T(8,128)(2,1)S(1)}, bf16[384,128]{0,1:T(8,128)(2,1)}, u32[]{:S(2)}) copy-start(bf16[384,128]{0,1:T(8,128)(2,1)} %copy.45) | copy-start | bytes 294916
  (15 other events, 23.1 us)
Sparse Core Ops, SparseCore 0:
  139.2 92.8 all-reduce.2
Sparse Core Ops, SparseCore 1:
  174.5 31.9 reduce-scatter.3
where the time goes:
time: 271 us; the launch traced here: 270 us
  other arithmetic  88.5 us (33%)
  local copies, waits for them, and re-layouts  71.4 us (26%)
  blocking collectives  49.3 us (18%)
  waiting for transfers between devices  20.9 us (8%)
  matrix products  17.1 us (6%)
  between operations  16.6 us (6%)
  starting transfers between devices  6.6 us (2%)
    psum x1, blocking collectives, per_device(): lax.psum((grad_edge_in, grad_edge_out, grad_node_in, grad_node_out, vecto...  31.8 us
    scatter-add x1, other arithmetic, local_layer(): jax.ops.segment_sum(d_edge_inputs[:, 2 * width:], receiver_ids, num_segme...  22.9 us
    scatter-add x1, other arithmetic, local_layer(): jax.ops.segment_sum(live_mask * edge_new, receiver_ids, num_segments=node...  22.9 us
    scatter-add x1, other arithmetic, local_layer(): jax.ops.segment_sum(d_edge_inputs[:, width:2 * width], sender_ids, num_se...  21.1 us
    gather x2, local copies, waits for them, and re-layouts, local_layer(): d_gathered[receiver_ids]  18.3 us
    all_gather x1, blocking collectives, per_device(): lax.all_gather(node_features, ('feat', 'sub'), axis=0, tiled=True)  17.6 us
    psum x1, waiting for transfers between devices, per_device(): lax.psum((grad_edge_in, grad_edge_out, grad_node_in, grad_node_out, vecto...  17.1 us
    unnamed x77, local copies, waits for them, and re-layouts  17.1 us
  transfers between devices with their start and end apart: 4, of which 2 were waited for; matrix products, arithmetic and copies ran while one was open for 23% of the time, Pallas kernels for 0%

commit v1 on v0

v1 whole, which is shorter than its diff:
```python
import functools

import jax
import jax.numpy as jnp
from jax import lax
from jax.experimental import pallas as pl
from jax.experimental.pallas import tpu as pltpu
from jax.sharding import PartitionSpec as P

epsilon = 1e-05
TILE = 512
F32 = jnp.float32
BF16 = jnp.bfloat16


def dot(a, b, ca=1, cb=0):
    return lax.dot_general(a, b, (((ca,), (cb,)), ((), ())), preferred_element_type=F32)


def sigmoid_of(x):
    return 0.5 * jnp.tanh(0.5 * x) + 0.5


def split(x):
    high = x.astype(BF16)
    low = (x - high.astype(F32)).astype(BF16)
    return jnp.concatenate([high, low], axis=1)


def mean(x):
    return jnp.mean(x, axis=-1, keepdims=True)


def forward(preact, w_out):
    hidden = (preact * sigmoid_of(preact)).astype(BF16)
    output = dot(hidden, w_out)
    centred = output - mean(output)
    inverse = lax.rsqrt(mean(centred * centred) + epsilon)
    return hidden, centred * inverse, inverse


def backward(r, preact, normed, inverse, w_out, gain):
    dn = r * gain
    d_output = inverse * (dn - mean(dn) - normed * mean(dn * normed))
    d_output_b = d_output.astype(BF16)
    d_hidden = dot(d_output_b, w_out, 1, 1)
    sig = sigmoid_of(preact)
    d_preact = d_hidden * sig * (1.0 + preact * (1.0 - sig))
    return d_output_b, d_preact


def down_rows(row):
    width = row.shape[1]
    return jnp.concatenate(
        [jnp.broadcast_to(row[:, c : c + 128], (128, 128)).T for c in range(0, width, 128)], axis=0
    )


def mark(hit):
    return jnp.where(hit, 1.0, 0.0).astype(BF16)


def layer_kernel(
    part_ref,
    halo_ref,
    node_ref,
    ncot_ref,
    ef_ref,
    ec_ref,
    snd_ref,
    rcv_ref,
    live_ref,
    ew1_ref,
    ew2_ref,
    evec_ref,
    nw1_ref,
    nw2_ref,
    nvec_ref,
    edge_out,
    node_out,
    sums_out,
    halo_out,
    terms_out,
    table,
    pair_table,
    slots_r,
    others,
    preacts,
    hiddens,
    normeds,
    inverses,
    gathered,
    acc,
    acc_rh,
):
    part_rows, width = part_ref.shape
    nodes = node_ref.shape[0]
    halos = halo_ref.shape[0]
    rows = table.shape[0]
    groups = part_rows // rows
    tiles = snd_ref.shape[0]
    live = live_ref[0]

    for g in range(groups):
        table[:, g * width : (g + 1) * width] = part_ref[g * rows : (g + 1) * rows, :]
    pair_table[0:nodes, 0:width] = node_ref[...]
    pair_table[0:nodes, width:] = jnp.zeros((nodes, width), BF16)
    pair_table[nodes:, 0:width] = jnp.zeros((halos, width), BF16)
    pair_table[nodes:, width:] = halo_ref[...]
    gathered[...] = jnp.zeros_like(gathered)
    acc[...] = jnp.zeros_like(acc)
    acc_rh[...] = jnp.zeros_like(acc_rh)
    terms_out[...] = jnp.zeros_like(terms_out)

    lane = lax.broadcasted_iota(jnp.int32, (TILE, 128), 1)
    deep = lax.broadcasted_iota(jnp.int32, (TILE, 128), 0)

    def group_of(s):
        group = jnp.zeros_like(s)
        for g in range(1, groups + 1):
            group = group + jnp.where(s >= g * rows, 1, 0)
        return group

    def ahead(i, _):
        here = pl.ds(pl.multiple_of(i * TILE, TILE), TILE)
        snd = snd_ref[i]
        s = down_rows(snd)
        r = down_rows(rcv_ref[i])
        group = group_of(s)
        low = s - group * rows
        far = s - part_rows
        low_hot = jnp.concatenate([mark(low == lane + j) for j in range(0, rows, 128)], axis=1)
        r_hot = jnp.concatenate([mark(r == lane + j) for j in range(0, nodes, 128)], axis=1)
        far_hot = jnp.concatenate([mark(far == lane + j) for j in range(0, halos, 128)], axis=1)
        slots_r[here, :] = r_hot
        picked = dot(low_hot, table[...])
        both = dot(jnp.concatenate([r_hot, far_hot], axis=1), pair_table[...])
        sent = both[:, width:]
        for g in range(groups):
            sent = jnp.where(group == g, picked[:, g * width : (g + 1) * width], sent)
        other = jnp.concatenate([sent.astype(BF16), both[:, :width].astype(BF16)], axis=1)
        others[here, :] = other
        ef = ef_ref[here, :]
        preact = dot(jnp.concatenate([ef, other], axis=1), ew1_ref[...]) + evec_ref[0:1, :]
        hidden, normed, inverse = forward(preact, ew2_ref[...])
        preacts[here, :] = preact
        hiddens[here, :] = hidden
        normeds[here, :] = normed
        inverses[here, :] = jnp.broadcast_to(inverse, (TILE, width))
        new = ef.astype(F32) + normed * evec_ref[1:2, :] + evec_ref[2:3, :]
        new = jnp.where(deep + i * TILE < live, new, 0.0)
        gathered[...] += dot(r_hot, split(new), 0, 0)
        return 0

    lax.fori_loop(0, tiles, ahead, 0)

    whole = gathered[:, :width] + gathered[:, width:]
    node_inputs = jnp.concatenate([node_ref[...], whole.astype(BF16)], axis=1)
    preact = dot(node_inputs, nw1_ref[...]) + nvec_ref[0:1, :]
    hidden, normed, inverse = forward(preact, nw2_ref[...])
    r = ncot_ref[...].astype(F32)
    d_output_b, d_preact = backward(r, preact, normed, inverse, nw2_ref[...], nvec_ref[1:2, :])
    d_preact_b = d_preact.astype(BF16)
    e1 = 3 * width
    e2 = e1 + width
    n1 = e2 + 2 * width
    n2 = n1 + width
    terms_out[e2:n1, :] = dot(node_inputs, d_preact_b, 0, 0)
    terms_out[n1:n2, :] = dot(hidden, d_output_b, 0, 0)
    terms_out[n2 + 3 : n2 + 4, :] = jnp.sum(d_preact, axis=0, keepdims=True)
    terms_out[n2 + 4 : n2 + 5, :] = jnp.sum(r * normed, axis=0, keepdims=True)
    terms_out[n2 + 5 : n2 + 6, :] = jnp.sum(r, axis=0, keepdims=True)
    d_inputs = dot(d_preact_b, nw1_ref[...], 1, 1)
    node_out[...] = r + d_inputs[:, :width]
    spread = split(d_inputs[:, width:])

    low_deep = lax.broadcasted_iota(jnp.int32, (rows, TILE), 0)
    node_deep = lax.broadcasted_iota(jnp.int32, (nodes, TILE), 0)
    halo_deep = lax.broadcasted_iota(jnp.int32, (halos, TILE), 0)

    def back(i, carried):
        sum_b, sum_g, sum_s = carried
        here = pl.ds(pl.multiple_of(i * TILE, TILE), TILE)
        snd = snd_ref[i]
        rcv = rcv_ref[i]
        group = group_of(snd)
        low_hot = mark(low_deep == snd - group * rows)
        r_hot = mark(node_deep == rcv)
        far_hot = mark(halo_deep == snd - part_rows)
        alive = deep + i * TILE < live
        dg = dot(slots_r[here, :], spread)
        dg = dg[:, :width] + dg[:, width:]
        total = ec_ref[here, :].astype(F32) + jnp.where(alive, dg, 0.0)
        r = jnp.where(alive, total, 0.0)
        normed = normeds[here, :]
        d_output_b, d_preact = backward(
            r, preacts[here, :], normed, inverses[here, :], ew2_ref[...], evec_ref[1:2, :]
        )
        d_preact_b = d_preact.astype(BF16)
        edge_out[here, :] = total + dot(d_preact_b, ew1_ref[0:width, :], 1, 1)
        inputs = jnp.concatenate([ef_ref[here, :], others[here, :]], axis=1)
        terms_out[0:e1, :] += dot(inputs, d_preact_b, 0, 0)
        terms_out[e1:e2, :] += dot(hiddens[here, :], d_output_b, 0, 0)
        down = group_of(down_rows(snd))
        zero = jnp.zeros_like(d_preact)
        placed = jnp.concatenate(
            [jnp.where(down == g, d_preact, zero).astype(BF16) for g in range(groups)], axis=1
        )
        acc[...] += dot(low_hot, placed)
        acc_rh[...] += dot(jnp.concatenate([r_hot, far_hot], axis=0), d_preact_b)
        return (
            sum_b + jnp.sum(d_preact, axis=0, keepdims=True),
            sum_g + jnp.sum(r * normed, axis=0, keepdims=True),
            sum_s + jnp.sum(r, axis=0, keepdims=True),
        )

    none = jnp.zeros((1, width), F32)
    sum_b, sum_g, sum_s = lax.fori_loop(0, tiles, back, (none, none, none))
    terms_out[n2 : n2 + 1, :] = sum_b
    terms_out[n2 + 1 : n2 + 2, :] = sum_g
    terms_out[n2 + 2 : n2 + 3, :] = sum_s
    for g in range(groups):
        sums_out[g * rows : (g + 1) * rows, :] = acc[:, g * width : (g + 1) * width].astype(BF16)
    halo_out[...] = acc_rh[nodes:, :].astype(BF16)
    node_out[...] += dot(acc_rh[0:nodes, :].astype(BF16), ew1_ref[2 * width :, :], 1, 1)


def layer(part, halo, node_rows, node_cot, edge_rows, edge_cot, senders, receivers, live, params):
    ew1, ew2, eb, eg, es, nw1, nw2, nb, ng = params
    edges, width = edge_rows.shape
    nodes = node_rows.shape[0]
    halos = halo.shape[0]
    rows = 2 * nodes
    groups = part.shape[0] // rows
    tiles = edges // TILE
    evec = jnp.stack([eb, eg, es])
    nvec = jnp.stack([nb, ng])
    terms = 7 * width + 8
    vmem = pl.BlockSpec(memory_space=pltpu.VMEM)
    smem = pl.BlockSpec(memory_space=pltpu.SMEM)
    return pl.pallas_call(
        layer_kernel,
        out_shape=(
            jax.ShapeDtypeStruct((edges, width), F32),
            jax.ShapeDtypeStruct((nodes, width), F32),
            jax.ShapeDtypeStruct(part.shape, BF16),
            jax.ShapeDtypeStruct(halo.shape, BF16),
            jax.ShapeDtypeStruct((terms, width), F32),
        ),
        in_specs=[vmem] * 8 + [smem] + [vmem] * 6,
        out_specs=[vmem] * 5,
        scratch_shapes=[
            pltpu.VMEM((rows, groups * width), BF16),
            pltpu.VMEM((nodes + halos, 2 * width), BF16),
            pltpu.VMEM((edges, nodes), BF16),
            pltpu.VMEM((edges, 2 * width), BF16),
            pltpu.VMEM((edges, width), F32),
            pltpu.VMEM((edges, width), BF16),
            pltpu.VMEM((edges, width), F32),
            pltpu.VMEM((edges, width), F32),
            pltpu.VMEM((nodes, 2 * width), F32),
            pltpu.VMEM((rows, groups * width), F32),
            pltpu.VMEM((nodes + halos, width), F32),
        ],
        compiler_params=pltpu.CompilerParams(vmem_limit_bytes=56 * 2**20),
        cost_estimate=pl.CostEstimate(
            flops=2 * edges * width * 10000, bytes_accessed=8 * 2**20, transcendentals=0
        ),
    )(
        part,
        halo,
        node_rows,
        node_cot,
        edge_rows,
        edge_cot,
        senders.reshape(tiles, 1, TILE),
        receivers.reshape(tiles, 1, TILE),
        live,
        ew1,
        ew2,
        evec,
        nw1,
        nw2,
        nvec,
    )


def per_device(
    node_features,
    edge_features,
    node_cotangent,
    edge_cotangent,
    senders,
    receivers,
    send_rows,
    live_edges,
    *params,
):
    slices = lax.axis_size(("feat", "sub"))
    partition = lax.all_gather(node_features, ("feat", "sub"), axis=0, tiled=True)
    node_part, width = partition.shape
    row_lists = send_rows[0]
    peers, per_peer = row_lists.shape
    outgoing = partition[row_lists]
    arrived = lax.all_to_all(outgoing, "graph", split_axis=0, concat_axis=0, tiled=True)
    edge_grads, node_base, sums, halo_sums, terms = layer(
        partition,
        arrived.reshape(peers * per_peer, width),
        node_features,
        node_cotangent,
        edge_features,
        edge_cotangent,
        senders,
        receivers,
        live_edges,
        params,
    )
    summed = lax.psum(terms, ("graph", "feat", "sub"))
    returned = lax.all_to_all(
        halo_sums.reshape(peers, per_peer, width), "graph", split_axis=0, concat_axis=0, tiled=True
    )
    hot = (
        row_lists.reshape(1, -1) == jnp.arange(node_part, dtype=jnp.int32)[:, None]
    ).astype(BF16)
    partial_value = sums.astype(F32) + dot(hot, returned.reshape(-1, width))
    own = lax.psum_scatter(
        partial_value.astype(BF16), ("feat", "sub"), scatter_dimension=0, tiled=True
    )
    node_total = node_base + dot(own, params[0][width : 2 * width], 1, 1)
    device_count = lax.axis_size("graph") * slices
    edge_scale = float(device_count * edge_features.shape[0]) ** (-0.5)
    node_scale = float(device_count * node_features.shape[0]) ** (-0.5)
    row_scales = jnp.array([edge_scale] * 3 + [node_scale] * 3, F32)[:, None]
    e1, e2, n1, n2 = 3 * width, 4 * width, 6 * width, 7 * width
    return (
        node_total,
        edge_grads,
        summed[:e1] * edge_scale,
        summed[e1:e2] * edge_scale,
        summed[e2:n1] * node_scale,
        summed[n1:n2] * node_scale,
        summed[n2 : n2 + 6] * row_scales,
    )


def solution(mesh):
    everywhere = ("groups", "graph", "feat", "sub")
    in_specs = (
        P(everywhere, None),
        P(everywhere, None),
        P(everywhere, None),
        P(everywhere, None),
        P(everywhere),
        P(everywhere),
        P(("groups", "graph"), None, None),
        P(everywhere),
    ) + (P(),) * 9
    out_specs = (
        P(everywhere, None),
        P(everywhere, None),
    ) + (P("groups", None),) * 5
    return jax.shard_map(
        per_device, mesh=mesh, in_specs=in_specs, out_specs=out_specs, check_vma=False
    )
```

time: 271 us -> 182 us (0.67)
  other arithmetic: 88.5 us -> 9.27 us
  waiting for transfers between devices: 20.9 us -> 95.3 us
  local copies, waits for them, and re-layouts: 71.4 us -> 2.1 us
  blocking collectives: 49.3 us -> 17.4 us
  Pallas kernels: 0 us -> 30.4 us
  matrix products: 17.1 us -> 4.3 us
    psum x1, waiting for transfers between devices: 17.1 us -> 90.8 us  [per_device(): summed = lax.psum(terms, ('graph', 'feat', 'sub'))]
    scatter-add x4 -> x0, other arithmetic: 68.7 us -> none  [the longest x1 22.9 us: local_layer(): jax.ops.segment_sum(d_edge_inputs[:, 2 * width:], receiver_ids, num_segme...]
    gather x4 -> x0, local copies, waits for them, and re-layouts: 45.5 us -> none  [the longest x2 18.3 us: local_layer(): d_gathered[receiver_ids]]
    psum x1 -> x0, blocking collectives: 31.8 us -> none  [per_device(): lax.psum((grad_edge_in, grad_edge_out, grad_node_in, grad_node_out, vecto...]
    pallas_call x0 -> x1, Pallas kernels: none -> 30.4 us  [layer(): pl.pallas_call(layer_kernel, out_shape=(jax.ShapeDtypeStruct((edges, widt...]
    unnamed x77 -> x10, local copies, waits for them, and re-layouts: 17.1 us -> 0.63 us
    dot_general x12 -> x2, matrix products: 17.1 us -> 4.3 us  [dot(): lax.dot_general(a, b, (((ca,), (cb,)), ((), ())), preferred_element_type=...]
    reduce_sum x4 -> x0, other arithmetic: 4.65 us -> none  [the longest x2 4.37 us: mlp_backward(): jnp.sum(d_result * normed, axis=0)]
  transfers between devices with their start and end apart: 4 -> 4, of which waited for: 2 -> 3; matrix products, arithmetic and copies ran while one was open for 23% -> 6% of each run, Pallas kernels for 0% -> 0%
where the time goes in v1:
time: 182 us
  waiting for transfers between devices  95.3 us (52%)
  Pallas kernels  30.4 us (17%)
  blocking collectives  17.4 us (10%)
  between operations  16.2 us (9%)
  other arithmetic  9.27 us (5%)
  starting transfers between devices  6.61 us (4%)
  matrix products  4.3 us (2%)
  local copies, waits for them, and re-layouts  2.1 us (1%)
    psum x1, waiting for transfers between devices, per_device(): summed = lax.psum(terms, ('graph', 'feat', 'sub'))  90.8 us
    pallas_call x1, Pallas kernels, layer(): pl.pallas_call(layer_kernel, out_shape=(jax.ShapeDtypeStruct((edges, widt...  30.4 us
    all_gather x1, blocking collectives, per_device(): lax.all_gather(node_features, ('feat', 'sub'), axis=0, tiled=True)  17.4 us
    dot_general x2, matrix products, dot(): lax.dot_general(a, b, (((ca,), (cb,)), ((), ())), preferred_element_type=...  4.3 us
  transfers between devices with their start and end apart: 4, of which 3 were waited for; matrix products, arithmetic and copies ran while one was open for 6% of the time, Pallas kernels for 0%

profile of v1, /device:TPU:0, one launch (start us, length us, event | category | flops | bytes accessed | tf_op | source)
XLA Modules:
  0.0 181.6 jit_solution(2294502390843379592)
XLA Ops:
  8.0 17.4 %all_gather.3.part_ref = bf16[3072,128]{1,0:T(8,128)(2,1)S(1)} all-gather(bf16[384,128]{1,0:T(8,128)(2,1)} %node_ref.1), channel_id=1, replica_groups=mesh['groups'=2,'graph'=2,'feat'=4,'sub'=2] {'feat','sub'}, dimensions={0}, use_global_device_ids=true | all-gather | bytes 884736 | tf_op jit(solution)/shard_map/all_gather | solution.py:300
  25.4 0.7 compare_select_fusion
  26.1 0.1 reshape.66
  26.2 1.3 gather_fusion
  27.5 3.3 %all-to-all-start = ((bf16[2,64,128]{2,1,0:T(8,128)(2,1)}), bf16[2,64,128]{2,1,0:T(8,128)(2,1)S(1)}, u32[]{:S(2)}, u32[]{:S(2)}) async-start(bf16[2,64,128]{2,1,0:T(8,128)(2,1)} %bitcast.1), calls=%async_computation | async-start | bytes 65536 | tf_op jit(solution)/shard_map/all_to_all | solution.py:305
  30.8 1.3 pad_maximum_fusion.evec_ref
  32.1 1.2 pad_maximum_fusion.1.nvec_ref
  34.0 0.8 all-to-all-done
  34.7 0.6 copy-done.2
  35.3 30.4 %shard_map.225 = (f32[4096,128]{1,0:T(8,128)}, f32[384,128]{1,0:T(8,128)}, bf16[3072,128]{1,0:T(8,128)(2,1)}, bf16[128,128]{1,0:T(8,128)(2,1)}, f32[904,128]{1,0:T(8,128)}) custom-call(bf16[3072,128]{1,0:T(8,128)(2,1)} %copy-done, bf16[128,128]{1,0:T(8,128)(2,1)} %bitcast.19, bf16[384,128]{1,0:T(8,128)(2,1)} %node_ref.1, bf16[384,128]{1,0:T(8,128)(2,1)} %ncot_ref.1, ...), custom_call_target="tpu_custom_call" | custom-call | flops 10485760000 | bytes 8388608 | tf_op jit(solution)/shard_map/pallas_call | solution.py:241
  65.8 3.3 %all-to-all-start.1 = ((bf16[2,64,128]{2,1,0:T(8,128)(2,1)}), bf16[2,64,128]{2,1,0:T(8,128)(2,1)S(1)}, u32[]{:S(2)}, u32[]{:S(2)}) async-start(bf16[2,64,128]{2,1,0:T(8,128)(2,1)} %bitcast.18), calls=%async_computation.1 | async-start | bytes 65536 | tf_op jit(solution)/shard_map/all_to_all | solution.py:319
  69.1 0.0 all-reduce.2.cloned.1.call-start
  69.1 0.1 eq.15
  69.2 0.6 all-reduce.2.cloned.1.call-update
  69.8 0.0 reduce-scatter.2.cloned.1.call-start
  69.9 3.1 %all-to-all-done.1 = bf16[2,64,128]{2,1,0:T(8,128)(2,1)S(1)} async-done(((bf16[2,64,128]{2,1,0:T(8,128)(2,1)}), bf16[2,64,128]{2,1,0:T(8,128)(2,1)S(1)}, u32[]{:S(2)}, u32[]{:S(2)}) %all-to-all-start.1) | async-done | bytes 32800 | tf_op jit(solution)/shard_map/all_to_all | solution.py:319
  73.0 2.5 %fusion = bf16[3072,128]{1,0:T(8,128)(2,1)} fusion(bf16[128,128]{1,0:T(8,128)(2,1)S(1)} %bitcast.17, bf16[3072,128]{1,0:T(8,128)(2,1)} %get-tuple-element.13, s32[128]{0:T(128)S(1)} %eq.15), kind=kOutput, calls=%fused_computation.2 | convolution fusion | flops 102236160 | bytes 1606144 | tf_op jit(solution)/shard_map/dot_general | solution.py:17
  75.5 0.0 reduce-scatter.2.cloned.1.call-update
  75.6 90.8 %all-reduce.2.cloned.1.call-done = f32[904,128]{1,0:T(8,128)} async-done(((f32[904,128]{1,0:T(8,128)}), f32[904,128]{1,0:T(8,128)}) %all-reduce.2.cloned.1.call-update) | async-done | bytes 462864 | tf_op jit(solution)/shard_map/psum | solution.py:318
  166.4 1.3 slice_multiply_fusion.4
  167.7 1.5 slice_multiply_fusion.2
  169.2 1.6 slice_multiply_fusion.1
  170.8 1.6 slice_multiply_fusion
  172.4 1.8 convolution_add_fusion.1
  (11 shorter events, 0.0 us)
Async XLA Ops:
  25.4 9.3 %copy-start = (bf16[3072,128]{1,0:T(8,128)(2,1)}, bf16[3072,128]{1,0:T(8,128)(2,1)S(1)}, u32[]{:S(2)}) copy-start(bf16[3072,128]{1,0:T(8,128)(2,1)S(1)} %all_gather.3.part_ref) | copy-start | bytes 2359300
  27.5 7.2 %all-to-all-start = ((bf16[2,64,128]{2,1,0:T(8,128)(2,1)}), bf16[2,64,128]{2,1,0:T(8,128)(2,1)S(1)}, u32[]{:S(2)}, u32[]{:S(2)}) async-start(bf16[2,64,128]{2,1,0:T(8,128)(2,1)} %bitcast.1), calls=%async_computation | async-start | bytes 65536 | tf_op jit(solution)/shard_map/all_to_all | solution.py:305
  34.7 0.6 copy-start.2
  35.3 33.8 %copy-start.3 = (s32[1,2,64]{2,1,0:T(2,128)S(1)}, s32[1,2,64]{2,1,0:T(2,128)}, u32[]{:S(2)}) copy-start(s32[1,2,64]{2,1,0:T(2,128)} %param.24) | copy-start | bytes 1540
  65.8 100.6 %copy-start.4 = (f32[6]{0:T(128)S(1)}, f32[6]{0:T(128)}, u32[]{:S(2)}) copy-start(f32[6]{0:T(128)} %constant.3.clone) | copy-start | bytes 76
  65.8 7.2 %all-to-all-start.1 = ((bf16[2,64,128]{2,1,0:T(8,128)(2,1)}), bf16[2,64,128]{2,1,0:T(8,128)(2,1)S(1)}, u32[]{:S(2)}, u32[]{:S(2)}) async-start(bf16[2,64,128]{2,1,0:T(8,128)(2,1)} %bitcast.18), calls=%async_computation.1 | async-start | bytes 65536 | tf_op jit(solution)/shard_map/all_to_all | solution.py:319
  69.1 97.3 %all-reduce.2.cloned.1.call-start = ((), (), s32[]{:S(2)}) async-start(), calls=%async_computation.4 | async-start | bytes 925696 | tf_op jit(solution)/shard_map/psum | solution.py:318
  69.8 102.6 %reduce-scatter.2.cloned.1.call-start = ((), (), s32[]{:S(2)}) async-start(), calls=%async_computation.3 | async-start | bytes 884736 | tf_op jit(solution)/shard_map/reduce_scatter | solution.py:326
  73.0 99.4 %copy-start.1 = (f32[384,128]{1,0:T(8,128)S(1)}, f32[384,128]{1,0:T(8,128)}, u32[]{:S(2)}) copy-start(f32[384,128]{1,0:T(8,128)} %get-tuple-element.12) | copy-start | bytes 589828
Sparse Core Ops, SparseCore 0:
  73.7 92.6 all-reduce.1
Sparse Core Ops, SparseCore 1:
  75.6 31.9 reduce-scatter.1

commit v2 on v1

--- a/solution.py
+++ b/solution.py
@@ -93,8 +93,8 @@
     acc,
     acc_rh,
 ):
-    part_rows, width = part_ref.shape
-    nodes = node_ref.shape[0]
+    slots, nodes, width = part_ref.shape
+    part_rows = slots * nodes
     halos = halo_ref.shape[0]
     rows = table.shape[0]
     groups = part_rows // rows
@@ -102,7 +102,10 @@
     live = live_ref[0]
 
     for g in range(groups):
-        table[:, g * width : (g + 1) * width] = part_ref[g * rows : (g + 1) * rows, :]
+        for k in range(rows // nodes):
+            table[k * nodes : (k + 1) * nodes, g * width : (g + 1) * width] = part_ref[
+                g * (rows // nodes) + k
+            ]
     pair_table[0:nodes, 0:width] = node_ref[...]
     pair_table[0:nodes, width:] = jnp.zeros((nodes, width), BF16)
     pair_table[nodes:, 0:width] = jnp.zeros((halos, width), BF16)
@@ -220,22 +223,24 @@
     terms_out[n2 + 1 : n2 + 2, :] = sum_g
     terms_out[n2 + 2 : n2 + 3, :] = sum_s
     for g in range(groups):
-        sums_out[g * rows : (g + 1) * rows, :] = acc[:, g * width : (g + 1) * width].astype(BF16)
+        for k in range(rows // nodes):
+            sums_out[g * (rows // nodes) + k] = acc[
+                k * nodes : (k + 1) * nodes, g * width : (g + 1) * width
+            ].astype(BF16)
     halo_out[...] = acc_rh[nodes:, :].astype(BF16)
     node_out[...] += dot(acc_rh[0:nodes, :].astype(BF16), ew1_ref[2 * width :, :], 1, 1)
 
 
-def layer(part, halo, node_rows, node_cot, edge_rows, edge_cot, senders, receivers, live, params):
+def layer(part, halo, node_rows, node_cot, edge_rows, edge_cot, senders, receivers, live, params, terms):
     ew1, ew2, eb, eg, es, nw1, nw2, nb, ng = params
     edges, width = edge_rows.shape
     nodes = node_rows.shape[0]
     halos = halo.shape[0]
     rows = 2 * nodes
-    groups = part.shape[0] // rows
+    groups = part.shape[0] * part.shape[1] // rows
     tiles = edges // TILE
     evec = jnp.stack([eb, eg, es])
     nvec = jnp.stack([nb, ng])
-    terms = 7 * width + 8
     vmem = pl.BlockSpec(memory_space=pltpu.VMEM)
     smem = pl.BlockSpec(memory_space=pltpu.SMEM)
     return pl.pallas_call(
@@ -285,6 +290,324 @@
     )
 
 
+def greet(partners):
+    barrier = pltpu.get_barrier_semaphore()
+    for partner in partners:
+        pl.semaphore_signal(
+            barrier, inc=1, device_id=partner, device_id_type=pl.DeviceIdType.MESH
+        )
+    pl.semaphore_wait(barrier, len(partners))
+
+
+def push(src, dst, send, recv, partner):
+    return pltpu.make_async_remote_copy(
+        src_ref=src,
+        dst_ref=dst,
+        send_sem=send,
+        recv_sem=recv,
+        device_id=partner,
+        device_id_type=pl.DeviceIdType.MESH,
+    )
+
+
+def around(axis, count):
+    me = lax.axis_index(axis)
+    return [{axis: lax.rem(me + off, count)} for off in range(1, count)]
+
+
+def gather_kernel(
+    peers, feats, node_ref, rows_ref, part_ref, halo_ref, picked,
+    feat_send, feat_recv, sub_send, sub_recv, graph_send, graph_recv
+):
+    p = lax.axis_index("graph")
+    f = lax.axis_index("feat")
+    c = lax.axis_index("sub")
+    sibling = {"sub": 1 - c}
+    nodes = node_ref.shape[0]
+    halos = rows_ref.shape[1]
+    per = halos // peers
+    greet([sibling] + around("feat", feats) + around("graph", peers))
+    mine = 2 * f + c
+    started = []
+
+    def go(copy):
+        copy.start()
+        started.append(copy)
+
+    for off in range(feats - 1, 0, -1):
+        to = {"feat": lax.rem(f + off, feats)}
+        go(push(node_ref, part_ref.at[mine], feat_send.at[off], feat_recv.at[off], to))
+    go(push(node_ref, part_ref.at[mine], sub_send.at[0], sub_recv.at[0], sibling))
+    part_ref[mine] = node_ref[...]
+    for off in range(1, feats):
+        source = lax.rem(f + feats - off, feats)
+        slot = part_ref.at[2 * source + c]
+        push(node_ref, slot, feat_send.at[off], feat_recv.at[off], sibling).wait_recv()
+        go(push(slot, slot, sub_send.at[off], sub_recv.at[off], sibling))
+    for off in range(feats):
+        source = lax.rem(f + feats - off, feats)
+        slot = part_ref.at[2 * source + 1 - c]
+        push(slot, slot, sub_send.at[off], sub_recv.at[off], sibling).wait_recv()
+    deep = lax.broadcasted_iota(jnp.int32, (nodes, halos), 0)
+    listed = rows_ref[...]
+    chosen = jnp.zeros((halos, node_ref.shape[1]), F32)
+    for slot in range(2 * feats):
+        chosen = chosen + dot(mark(deep + slot * nodes == listed), part_ref[slot], 0, 0)
+    chosen = chosen.astype(BF16)
+    for q in range(peers):
+        picked[q] = chosen[q * per : (q + 1) * per, :]
+    for off in range(1, peers):
+        to = lax.rem(p + off, peers)
+        go(
+            push(
+                picked.at[to], halo_ref.at[p], graph_send.at[off], graph_recv.at[off],
+                {"graph": to},
+            )
+        )
+    halo_ref[p] = picked[p]
+    for off in range(1, peers):
+        source = lax.rem(p + peers - off, peers)
+        push(
+            picked.at[0], halo_ref.at[source], graph_send.at[off], graph_recv.at[off], sibling
+        ).wait_recv()
+    for copy in started:
+        copy.wait_send()
+
+
+def gather(node_rows, row_lists, feats):
+    nodes, width = node_rows.shape
+    peers, per = row_lists.shape
+    vmem = pl.BlockSpec(memory_space=pltpu.VMEM)
+    dma = pltpu.SemaphoreType.DMA
+    return pl.pallas_call(
+        functools.partial(gather_kernel, peers, feats),
+        out_shape=(
+            jax.ShapeDtypeStruct((2 * feats, nodes, width), BF16),
+            jax.ShapeDtypeStruct((peers, per, width), BF16),
+        ),
+        in_specs=[vmem] * 2,
+        out_specs=[vmem] * 2,
+        scratch_shapes=[
+            pltpu.VMEM((peers, per, width), BF16),
+            dma((feats,)),
+            dma((feats,)),
+            dma((feats,)),
+            dma((feats,)),
+            dma((peers,)),
+            dma((peers,)),
+        ],
+        compiler_params=pltpu.CompilerParams(
+            collective_id=0, has_side_effects=True, vmem_limit_bytes=32 * 2**20
+        ),
+    )(node_rows, row_lists.reshape(1, peers * per))
+
+
+def reduce_kernel(
+    peers, feats, edge_scale, node_scale,
+    sums_ref, halo_ref, rows_ref, terms_ref, base_ref, w1_ref,
+    node_out, ein_out, eout_out, nin_out, nout_out, vec_out,
+    narrow, first, second, third, mid, late, onward, result,
+    returned, paired, ready, arrived,
+    halo_send, halo_recv, pair_send, pair_recv, feat_send, feat_recv,
+    t_sub_send, t_sub_recv, t_graph_send, t_graph_recv, t_feat_send, t_feat_recv,
+    g_sub_send, g_sub_recv, g_graph_send, g_graph_recv, g_feat_send, g_feat_recv
+):
+    p = lax.axis_index("graph")
+    f = lax.axis_index("feat")
+    c = lax.axis_index("sub")
+    sibling = {"sub": 1 - c}
+    slots, nodes, width = sums_ref.shape
+    halos = rows_ref.shape[1]
+    per = halos // peers
+    across = [{"graph": to["graph"], "sub": 1 - c} for to in around("graph", peers)]
+    greet([sibling] + around("feat", feats) + around("graph", peers) + across)
+    started = []
+
+    def go(copy):
+        copy.start()
+        started.append(copy)
+
+    for off in range(1, peers):
+        to = lax.rem(p + off, peers)
+        for swap, core in enumerate((c, 1 - c)):
+            go(
+                push(
+                    halo_ref.at[to], returned.at[c, p],
+                    halo_send.at[swap, off], halo_recv.at[swap, off],
+                    {"graph": to, "sub": core},
+                )
+            )
+    go(push(halo_ref.at[p], returned.at[c, p], halo_send.at[1, 0], halo_recv.at[1, 0], sibling))
+    narrow[...] = terms_ref[...].astype(BF16)
+    go(push(narrow.at[1 - c], first, t_sub_send, t_sub_recv, sibling))
+    for off in range(feats - 1, -1, -1):
+        to = lax.rem(f + off, feats)
+        go(
+            push(
+                sums_ref.at[2 * to + 1 - c], paired.at[to], pair_send.at[to], pair_recv.at[to],
+                sibling,
+            )
+        )
+    returned[c, p] = halo_ref[p]
+
+    push(first, first, t_sub_send, t_sub_recv, sibling).wait_recv()
+    mid[...] = (terms_ref[c] + first[...].astype(F32)).astype(BF16)
+    for off in range(1, peers):
+        to = lax.rem(p + off, peers)
+        go(
+            push(
+                mid.at[to], second.at[p], t_graph_send.at[off], t_graph_recv.at[off],
+                {"graph": to},
+            )
+        )
+
+    for swap, core in enumerate((c, 1 - c)):
+        for off in range(1 - swap, peers):
+            piece = returned.at[core, lax.rem(p + peers - off, peers)]
+            push(
+                piece, piece, halo_send.at[swap, off], halo_recv.at[swap, off], sibling
+            ).wait_recv()
+    boundary = returned[...].reshape(2 * halos, width)
+    deep = lax.broadcasted_iota(jnp.int32, (nodes, 2 * halos), 0)
+    listed = jnp.concatenate([rows_ref[...], rows_ref[...]], axis=1)
+
+    def joined(owner):
+        push(
+            paired.at[owner], paired.at[owner], pair_send.at[owner], pair_recv.at[owner], sibling
+        ).wait_recv()
+        place = 2 * owner + c
+        extra = dot(mark(deep + place * nodes == listed), boundary)
+        return sums_ref[place].astype(F32) + paired[owner].astype(F32) + extra
+
+    for off in range(feats - 1, 0, -1):
+        to = lax.rem(f + off, feats)
+        ready[to] = joined(to).astype(BF16)
+        go(
+            push(
+                ready.at[to], arrived.at[f], feat_send.at[off], feat_recv.at[off], {"feat": to}
+            )
+        )
+    own = joined(f)
+
+    total = terms_ref[c, p] + first[p].astype(F32)
+    for off in range(1, peers):
+        source = lax.rem(p + peers - off, peers)
+        push(
+            second.at[source], second.at[source], t_graph_send.at[off], t_graph_recv.at[off],
+            sibling,
+        ).wait_recv()
+        total = total + second[source].astype(F32)
+    late[...] = total
+    onward[...] = total.astype(BF16)
+    for off in range(feats - 1, 0, -1):
+        to = lax.rem(f + off, feats)
+        go(
+            push(
+                onward.at[to], third.at[f], t_feat_send.at[off], t_feat_recv.at[off],
+                {"feat": to},
+            )
+        )
+    total = late[f]
+    for off in range(1, feats):
+        source = lax.rem(f + feats - off, feats)
+        push(
+            third.at[source], third.at[source], t_feat_send.at[off], t_feat_recv.at[off], sibling
+        ).wait_recv()
+        total = total + third[source].astype(F32)
+    result[c, p, f] = total.astype(BF16)
+    for off in range(1, feats):
+        to = lax.rem(f + off, feats)
+        piece = result.at[c, p, f]
+        go(push(piece, piece, g_feat_send.at[off], g_feat_recv.at[off], {"feat": to}))
+    for off in range(1, feats):
+        source = lax.rem(f + feats - off, feats)
+        piece = result.at[c, p, source]
+        push(piece, piece, g_feat_send.at[off], g_feat_recv.at[off], sibling).wait_recv()
+    for off in range(1, peers):
+        to = lax.rem(p + off, peers)
+        piece = result.at[c, p]
+        go(push(piece, piece, g_graph_send.at[off], g_graph_recv.at[off], {"graph": to}))
+    for off in range(1, peers):
+        source = lax.rem(p + peers - off, peers)
+        piece = result.at[c, source]
+        push(piece, piece, g_graph_send.at[off], g_graph_recv.at[off], sibling).wait_recv()
+    go(push(result.at[c], result.at[c], g_sub_send, g_sub_recv, sibling))
+
+    for off in range(1, feats):
+        source = lax.rem(f + feats - off, feats)
+        push(
+            arrived.at[source], arrived.at[source], feat_send.at[off], feat_recv.at[off], sibling
+        ).wait_recv()
+        own = own + arrived[source].astype(F32)
+    node_out[...] = base_ref[...] + dot(own.astype(BF16), w1_ref[width : 2 * width, :], 1, 1)
+
+    other = result.at[1 - c]
+    push(other, other, g_sub_send, g_sub_recv, sibling).wait_recv()
+    block = result.shape[3]
+    e1, e2, n1, n2 = 3 * width, 4 * width, 6 * width, 7 * width
+    whole = result[...].reshape(2 * peers * feats * block, width).astype(F32)
+    ein_out[...] = whole[:e1] * edge_scale
+    eout_out[...] = whole[e1:e2] * edge_scale
+    nin_out[...] = whole[e2:n1] * node_scale
+    nout_out[...] = whole[n1:n2] * node_scale
+    vec_out[0:3, :] = whole[n2 : n2 + 3] * edge_scale
+    vec_out[3:6, :] = whole[n2 + 3 : n2 + 6] * node_scale
+    for copy in started:
+        copy.wait_send()
+
+
+def reduce(sums, halo_sums, row_lists, terms, base, w1, edge_scale, node_scale):
+    slots, nodes, width = sums.shape
+    feats = slots // 2
+    peers, per = row_lists.shape
+    block = terms.shape[0] // (2 * peers * feats)
+    vmem = pl.BlockSpec(memory_space=pltpu.VMEM)
+    dma = pltpu.SemaphoreType.DMA
+    out = [nodes, 3 * width, width, 2 * width, width, 6]
+    by_feat = [dma((feats,)), dma((feats,))]
+    by_peer = [dma((peers,)), dma((peers,))]
+    single = [dma, dma]
+    return pl.pallas_call(
+        functools.partial(reduce_kernel, peers, feats, edge_scale, node_scale),
+        out_shape=tuple(jax.ShapeDtypeStruct((rows, width), F32) for rows in out),
+        in_specs=[vmem] * 6,
+        out_specs=[vmem] * 6,
+        scratch_shapes=[
+            pltpu.VMEM((2, peers, feats, block, width), BF16),
+            pltpu.VMEM((peers, feats, block, width), BF16),
+            pltpu.VMEM((peers, feats, block, width), BF16),
+            pltpu.VMEM((feats, block, width), BF16),
+            pltpu.VMEM((peers, feats, block, width), BF16),
+            pltpu.VMEM((feats, block, width), F32),
+            pltpu.VMEM((feats, block, width), BF16),
+            pltpu.VMEM((2, peers, feats, block, width), BF16),
+            pltpu.VMEM((2, peers, per, width), BF16),
+            pltpu.VMEM((feats, nodes, width), BF16),
+            pltpu.VMEM((feats, nodes, width), BF16),
+            pltpu.VMEM((feats, nodes, width), BF16),
+        ]
+        + [dma((2, peers)), dma((2, peers))]
+        + by_feat
+        + by_feat
+        + single
+        + by_peer
+        + by_feat
+        + single
+        + by_peer
+        + by_feat,
+        compiler_params=pltpu.CompilerParams(
+            collective_id=1, has_side_effects=True, vmem_limit_bytes=32 * 2**20
+        ),
+    )(
+        sums,
+        halo_sums,
+        row_lists.reshape(1, peers * per),
+        terms.reshape(2, peers, feats, block, width),
+        base,
+        w1,
+    )
+
+
 def per_device(
     node_features,
     edge_features,
@@ -296,16 +619,17 @@
     live_edges,
     *params,
 ):
-    slices = lax.axis_size(("feat", "sub"))
-    partition = lax.all_gather(node_features, ("feat", "sub"), axis=0, tiled=True)
-    node_part, width = partition.shape
+    peers = lax.axis_size("graph")
+    feats = lax.axis_size("feat")
     row_lists = send_rows[0]
-    peers, per_peer = row_lists.shape
-    outgoing = partition[row_lists]
-    arrived = lax.all_to_all(outgoing, "graph", split_axis=0, concat_axis=0, tiled=True)
+    per = row_lists.shape[1]
+    nodes, width = node_features.shape
+    unit = 2 * peers * feats * 16
+    term_rows = -(-(7 * width + 8) // unit) * unit
+    partition, arrived = gather(node_features, row_lists, feats)
     edge_grads, node_base, sums, halo_sums, terms = layer(
         partition,
-        arrived.reshape(peers * per_peer, width),
+        arrived.reshape(peers * per, width),
         node_features,
         node_cotangent,
         edge_features,
@@ -314,33 +638,22 @@
         receivers,
         live_edges,
         params,
+        term_rows,
     )
-    summed = lax.psum(terms, ("graph", "feat", "sub"))
-    returned = lax.all_to_all(
-        halo_sums.reshape(peers, per_peer, width), "graph", split_axis=0, concat_axis=0, tiled=True
+    device_count = peers * feats * 2
+    edge_scale = float(device_count * edge_features.shape[0]) ** (-0.5)
+    node_scale = float(device_count * nodes) ** (-0.5)
+    node_total, ein, eout, nin, nout, vectors = reduce(
+        sums,
+        halo_sums.reshape(peers, per, width),
+        row_lists,
+        terms,
+        node_base,
+        params[0],
+        edge_scale,
+        node_scale,
     )
-    hot = (
-        row_lists.reshape(1, -1) == jnp.arange(node_part, dtype=jnp.int32)[:, None]
-    ).astype(BF16)
-    partial_value = sums.astype(F32) + dot(hot, returned.reshape(-1, width))
-    own = lax.psum_scatter(
-        partial_value.astype(BF16), ("feat", "sub"), scatter_dimension=0, tiled=True
-    )
-    node_total = node_base + dot(own, params[0][width : 2 * width], 1, 1)
-    device_count = lax.axis_size("graph") * slices
-    edge_scale = float(device_count * edge_features.shape[0]) ** (-0.5)
-    node_scale = float(device_count * node_features.shape[0]) ** (-0.5)
-    row_scales = jnp.array([edge_scale] * 3 + [node_scale] * 3, F32)[:, None]
-    e1, e2, n1, n2 = 3 * width, 4 * width, 6 * width, 7 * width
-    return (
-        node_total,
-        edge_grads,
-        summed[:e1] * edge_scale,
-        summed[e1:e2] * edge_scale,
-        summed[e2:n1] * node_scale,
-        summed[n1:n2] * node_scale,
-        summed[n2 : n2 + 6] * row_scales,
-    )
+    return (node_total, edge_grads, ein, eout, nin, nout, vectors)
 
 
 def solution(mesh):

time: 182 us -> 88.8 us (0.49)
  waiting for transfers between devices: 95.3 us -> 0 us
  Pallas kernels: 30.4 us -> 73.7 us
  blocking collectives: 17.4 us -> 0 us
  between operations: 16.2 us -> 1.33 us
  local copies, waits for them, and re-layouts: 2.1 us -> 10.9 us
  other arithmetic: 9.27 us -> 2.51 us
  starting transfers between devices: 6.61 us -> 0 us
  matrix products: 4.3 us -> 0 us
    psum x1 -> x0, waiting for transfers between devices: 90.8 us -> none  [per_device(): summed = lax.psum(terms, ('graph', 'feat', 'sub'))]
    pallas_call x0 -> x2, Pallas kernels: none -> 43.2 us  [the longest x1 24.9 us: reduce(): pl.pallas_call(functools.partial(reduce_kernel, peers, feats, edge_scale,...]
    all_gather x1 -> x0, blocking collectives: 17.4 us -> none  [per_device(): lax.all_gather(node_features, ('feat', 'sub'), axis=0, tiled=True)]
    unnamed x10 -> x22, local copies, waits for them, and re-layouts: 0.63 us -> 10.1 us
    all_to_all x2 -> x0, starting transfers between devices: 6.53 us -> none  [the longest x1 3.27 us: per_device(): lax.all_to_all(halo_sums.reshape(peers, per_peer, width), 'graph', split_...]
    mul x4 -> x0, other arithmetic: 6.06 us -> none  [the longest x1 1.62 us: per_device(): summed[:e1] * edge_scale]
    dot_general x2 -> x0, matrix products: 4.3 us -> none  [dot(): lax.dot_general(a, b, (((ca,), (cb,)), ((), ())), preferred_element_type=...]
    all_to_all x2 -> x0, waiting for transfers between devices: 3.9 us -> none  [the longest x1 3.14 us: per_device(): lax.all_to_all(halo_sums.reshape(peers, per_peer, width), 'graph', split_...]
  transfers between devices with their start and end apart: 4 -> 0, of which waited for: 3 -> 0; matrix products, arithmetic and copies ran while one was open for 6% -> 0% of each run, Pallas kernels for 0% -> 0%
where the time goes in v2:
time: 88.8 us; the launch traced here: 88.4 us
  Pallas kernels  73.7 us (83%)
  local copies, waits for them, and re-layouts  10.9 us (12%)
  other arithmetic  2.51 us (3%)
  between operations  1.33 us (1%)
    pallas_call x1, Pallas kernels, layer(): pl.pallas_call(layer_kernel, out_shape=(jax.ShapeDtypeStruct((edges, widt...  30.5 us
    pallas_call x1, Pallas kernels, reduce(): pl.pallas_call(functools.partial(reduce_kernel, peers, feats, edge_scale,...  24.9 us
    pallas_call x1, Pallas kernels, gather(): pl.pallas_call(functools.partial(gather_kernel, peers, feats), out_shape=...  18.3 us
    unnamed x22, local copies, waits for them, and re-layouts  10.1 us

profile of v2, /device:TPU:0, one launch (start us, length us, event | category | flops | bytes accessed | tf_op | source)
XLA Modules:
  0.0 88.4 jit_solution(8255309491801702049)
XLA Ops:
  1.3 0.8 reshape_squeeze.4.rows_ref
  2.0 1.2 %pad_maximum_fusion.1.nvec_ref = f32[2,128]{1,0:T(2,128)} fusion(f32[1,128]{1,0:T(1,128)} %bitcast.16, f32[1,128]{1,0:T(1,128)} %bitcast.17), kind=kLoop, calls=%fused_computation.1 | loop fusion | flops 256 | bytes 2048 | tf_op jit(solution)/shard_map/stack | solution.py:243
  3.3 1.3 %pad_maximum_fusion.evec_ref = f32[3,128]{1,0:T(4,128)} fusion(f32[1,128]{1,0:T(1,128)} %bitcast.13, f32[1,128]{1,0:T(1,128)} %bitcast.14, f32[1,128]{1,0:T(1,128)} %bitcast.15), kind=kLoop, calls=%fused_computation | loop fusion | flops 768 | bytes 3072 | tf_op jit(solution)/shard_map/stack | solution.py:242
  4.6 0.0 copy-start.4
  4.6 0.9 %copy-done.4 = bf16[384,128]{1,0:T(8,128)(2,1)S(1)} copy-done((bf16[384,128]{1,0:T(8,128)(2,1)S(1)}, bf16[384,128]{1,0:T(8,128)(2,1)}, u32[]{:S(2)}) %copy-start.4) | copy-done | bytes 98328
  5.4 18.3 %shard_map.216 = (bf16[8,384,128]{2,1,0:T(8,128)(2,1)S(1)}, bf16[2,64,128]{2,1,0:T(8,128)(2,1)S(1)}) custom-call(bf16[384,128]{1,0:T(8,128)(2,1)S(1)} %copy-done.4, s32[1,128]{1,0:T(1,128)S(1)} %reshape_squeeze.4.rows_ref), custom_call_target="tpu_custom_call" | custom-call | tf_op jit(solution)/shard_map/pallas_call | solution.py:382
  23.7 0.0 copy-start.6
  23.7 0.9 copy-done.6
  24.6 0.0 copy-start.7
  24.6 0.6 copy-done.7
  25.2 30.5 %shard_map.217 = (f32[4096,128]{1,0:T(8,128)}, f32[384,128]{1,0:T(8,128)}, bf16[8,384,128]{2,1,0:T(8,128)(2,1)}, bf16[128,128]{1,0:T(8,128)(2,1)}, f32[1024,128]{1,0:T(8,128)}) custom-call(bf16[8,384,128]{2,1,0:T(8,128)(2,1)} %copy-done.6, bf16[128,128]{1,0:T(8,128)(2,1)} %bitcast.12, bf16[384,128]{1,0:T(8,128)(2,1)} %node_ref.3, bf16[384,128]{1,0:T(8,128)(2,1)} %ncot_ref.1, ...), custom_call_target="tpu_custom_call" | custom-call | flops 10485760000 | bytes 8388608 | tf_op jit(solution)/shard_map/pallas_call | solution.py:246
  55.7 0.0 copy-done.3
  55.7 0.0 copy-start
  55.8 1.1 %copy-done = bf16[8,384,128]{2,1,0:T(8,128)(2,1)S(1)} copy-done((bf16[8,384,128]{2,1,0:T(8,128)(2,1)S(1)}, bf16[8,384,128]{2,1,0:T(8,128)(2,1)}, u32[]{:S(2)}) %copy-start) | copy-done | bytes 786456
  56.9 1.0 %copy-done.1 = f32[1024,128]{1,0:T(8,128)S(1)} copy-done((f32[1024,128]{1,0:T(8,128)S(1)}, f32[1024,128]{1,0:T(8,128)}, u32[]{:S(2)}) %copy-start.1) | copy-done | bytes 524312
  57.9 0.9 %copy-done.2 = f32[384,128]{1,0:T(8,128)S(1)} copy-done((f32[384,128]{1,0:T(8,128)S(1)}, f32[384,128]{1,0:T(8,128)}, u32[]{:S(2)}) %copy-start.2) | copy-done | bytes 196632
  58.8 0.8 copy-done.5
  59.6 24.9 %shard_map.218 = (f32[384,128]{1,0:T(8,128)S(1)}, f32[384,128]{1,0:T(8,128)S(1)}, f32[128,128]{1,0:T(8,128)S(1)}, f32[256,128]{1,0:T(8,128)S(1)}, f32[128,128]{1,0:T(8,128)S(1)}, /*index=5*/f32[6,128]{1,0:T(8,128)S(1)}) custom-call(bf16[8,384,128]{2,1,0:T(8,128)(2,1)S(1)} %copy-done, bf16[2,64,128]{2,1,0:T(8,128)(2,1)S(1)} %bitcast.11, ...), custom_call_target="tpu_custom_call" | custom-call | tf_op jit(solution)/shard_map/pallas_call | solution.py:570
  84.5 0.7 copy.31
  85.2 0.7 copy.32
  85.9 0.6 copy.33
  86.5 0.7 copy.34
  87.2 0.6 copy.35
  87.8 0.6 copy.36
  (4 shorter events, 0.0 us)
Async XLA Ops:
  4.6 0.9 %copy-start.4 = (bf16[384,128]{1,0:T(8,128)(2,1)S(1)}, bf16[384,128]{1,0:T(8,128)(2,1)}, u32[]{:S(2)}) copy-start(bf16[384,128]{1,0:T(8,128)(2,1)} %node_ref.3) | copy-start | bytes 294916
  23.7 0.9 copy-start.6
  24.6 0.6 copy-start.7
  25.2 30.5 %copy-start.3 = (bf16[384,128]{1,0:T(8,128)(2,1)S(1)}, bf16[384,128]{1,0:T(8,128)(2,1)}, u32[]{:S(2)}) copy-start(bf16[384,128]{1,0:T(8,128)(2,1)} %w1_ref.1) | copy-start | bytes 294916
  55.7 1.1 %copy-start = (bf16[8,384,128]{2,1,0:T(8,128)(2,1)S(1)}, bf16[8,384,128]{2,1,0:T(8,128)(2,1)}, u32[]{:S(2)}) copy-start(bf16[8,384,128]{2,1,0:T(8,128)(2,1)} %get-tuple-element.22.sums_ref) | copy-start | bytes 2359300
  56.9 1.0 %copy-start.1 = (f32[1024,128]{1,0:T(8,128)S(1)}, f32[1024,128]{1,0:T(8,128)}, u32[]{:S(2)}) copy-start(f32[1024,128]{1,0:T(8,128)} %get-tuple-element.24) | copy-start | bytes 1572868
  57.9 0.9 %copy-start.2 = (f32[384,128]{1,0:T(8,128)S(1)}, f32[384,128]{1,0:T(8,128)}, u32[]{:S(2)}) copy-start(f32[384,128]{1,0:T(8,128)} %get-tuple-element.25.base_ref) | copy-start | bytes 589828
  58.8 0.8 copy-start.5

commit v3 on v2

--- a/solution.py
+++ b/solution.py
@@ -72,10 +72,13 @@
     live_ref,
     ew1_ref,
     ew2_ref,
-    evec_ref,
+    eb_ref,
+    eg_ref,
+    es_ref,
     nw1_ref,
     nw2_ref,
-    nvec_ref,
+    nb_ref,
+    ng_ref,
     edge_out,
     node_out,
     sums_out,
@@ -144,13 +147,13 @@
         other = jnp.concatenate([sent.astype(BF16), both[:, :width].astype(BF16)], axis=1)
         others[here, :] = other
         ef = ef_ref[here, :]
-        preact = dot(jnp.concatenate([ef, other], axis=1), ew1_ref[...]) + evec_ref[0:1, :]
+        preact = dot(jnp.concatenate([ef, other], axis=1), ew1_ref[...]) + eb_ref[...]
         hidden, normed, inverse = forward(preact, ew2_ref[...])
         preacts[here, :] = preact
         hiddens[here, :] = hidden
         normeds[here, :] = normed
         inverses[here, :] = jnp.broadcast_to(inverse, (TILE, width))
-        new = ef.astype(F32) + normed * evec_ref[1:2, :] + evec_ref[2:3, :]
+        new = ef.astype(F32) + normed * eg_ref[...] + es_ref[...]
         new = jnp.where(deep + i * TILE < live, new, 0.0)
         gathered[...] += dot(r_hot, split(new), 0, 0)
         return 0
@@ -159,10 +162,10 @@
 
     whole = gathered[:, :width] + gathered[:, width:]
     node_inputs = jnp.concatenate([node_ref[...], whole.astype(BF16)], axis=1)
-    preact = dot(node_inputs, nw1_ref[...]) + nvec_ref[0:1, :]
+    preact = dot(node_inputs, nw1_ref[...]) + nb_ref[...]
     hidden, normed, inverse = forward(preact, nw2_ref[...])
     r = ncot_ref[...].astype(F32)
-    d_output_b, d_preact = backward(r, preact, normed, inverse, nw2_ref[...], nvec_ref[1:2, :])
+    d_output_b, d_preact = backward(r, preact, normed, inverse, nw2_ref[...], ng_ref[...])
     d_preact_b = d_preact.astype(BF16)
     e1 = 3 * width
     e2 = e1 + width
@@ -197,7 +200,7 @@
         r = jnp.where(alive, total, 0.0)
         normed = normeds[here, :]
         d_output_b, d_preact = backward(
-            r, preacts[here, :], normed, inverses[here, :], ew2_ref[...], evec_ref[1:2, :]
+            r, preacts[here, :], normed, inverses[here, :], ew2_ref[...], eg_ref[...]
         )
         d_preact_b = d_preact.astype(BF16)
         edge_out[here, :] = total + dot(d_preact_b, ew1_ref[0:width, :], 1, 1)
@@ -239,8 +242,7 @@
     rows = 2 * nodes
     groups = part.shape[0] * part.shape[1] // rows
     tiles = edges // TILE
-    evec = jnp.stack([eb, eg, es])
-    nvec = jnp.stack([nb, ng])
+    eb, eg, es, nb, ng = (v.reshape(1, width) for v in (eb, eg, es, nb, ng))
     vmem = pl.BlockSpec(memory_space=pltpu.VMEM)
     smem = pl.BlockSpec(memory_space=pltpu.SMEM)
     return pl.pallas_call(
@@ -252,7 +254,7 @@
             jax.ShapeDtypeStruct(halo.shape, BF16),
             jax.ShapeDtypeStruct((terms, width), F32),
         ),
-        in_specs=[vmem] * 8 + [smem] + [vmem] * 6,
+        in_specs=[vmem] * 8 + [smem] + [vmem] * 9,
         out_specs=[vmem] * 5,
         scratch_shapes=[
             pltpu.VMEM((rows, groups * width), BF16),
@@ -283,10 +285,13 @@
         live,
         ew1,
         ew2,
-        evec,
+        eb,
+        eg,
+        es,
         nw1,
         nw2,
-        nvec,
+        nb,
+        ng,
     )
 
 

time: 88.8 us -> 86.3 us (0.972)
  other arithmetic: 2.51 us -> 0 us
    another operation x2 -> x0, other arithmetic: 2.51 us -> none  [the longest x1 1.27 us: layer(): evec = jnp.stack([eb, eg, es])]
where the time goes in v3:
time: 86.3 us; the launch traced here: 85.9 us
  Pallas kernels  73.8 us (86%)
  local copies, waits for them, and re-layouts  10.9 us (13%)
  between operations  1.33 us (2%)
    pallas_call x1, Pallas kernels, layer(): pl.pallas_call(layer_kernel, out_shape=(jax.ShapeDtypeStruct((edges, widt...  30.6 us
    pallas_call x1, Pallas kernels, reduce(): pl.pallas_call(functools.partial(reduce_kernel, peers, feats, edge_scale,...  24.9 us
    pallas_call x1, Pallas kernels, gather(): pl.pallas_call(functools.partial(gather_kernel, peers, feats), out_shape=...  18.3 us
    unnamed x22, local copies, waits for them, and re-layouts  10.1 us

profile of v3, /device:TPU:0, one launch (start us, length us, event | category | flops | bytes accessed | tf_op | source)
XLA Modules:
  0.0 85.9 jit_solution(18255626587885342264)
XLA Ops:
  1.3 0.8 reshape_squeeze.4.rows_ref
  2.0 0.0 copy-start.4
  2.0 0.9 %copy-done.4 = bf16[384,128]{1,0:T(8,128)(2,1)S(1)} copy-done((bf16[384,128]{1,0:T(8,128)(2,1)S(1)}, bf16[384,128]{1,0:T(8,128)(2,1)}, u32[]{:S(2)}) %copy-start.4) | copy-done | bytes 98328
  2.9 18.3 %shard_map.216 = (bf16[8,384,128]{2,1,0:T(8,128)(2,1)S(1)}, bf16[2,64,128]{2,1,0:T(8,128)(2,1)S(1)}) custom-call(bf16[384,128]{1,0:T(8,128)(2,1)S(1)} %copy-done.4, s32[1,128]{1,0:T(1,128)S(1)} %reshape_squeeze.4.rows_ref), custom_call_target="tpu_custom_call" | custom-call | tf_op jit(solution)/shard_map/pallas_call | solution.py:387
  21.2 0.0 copy-start.6
  21.2 0.9 %copy-done.6 = bf16[8,384,128]{2,1,0:T(8,128)(2,1)} copy-done((bf16[8,384,128]{2,1,0:T(8,128)(2,1)}, bf16[8,384,128]{2,1,0:T(8,128)(2,1)S(1)}, u32[]{:S(2)}) %copy-start.6) | copy-done | bytes 786456
  22.1 0.0 copy-start.7
  22.1 0.6 copy-done.7
  22.7 0.0 copy-start.3
  22.7 30.6 %shard_map.217 = (f32[4096,128]{1,0:T(8,128)}, f32[384,128]{1,0:T(8,128)}, bf16[8,384,128]{2,1,0:T(8,128)(2,1)}, bf16[128,128]{1,0:T(8,128)(2,1)}, f32[1024,128]{1,0:T(8,128)}) custom-call(bf16[8,384,128]{2,1,0:T(8,128)(2,1)} %copy-done.6, bf16[128,128]{1,0:T(8,128)(2,1)} %bitcast.12, bf16[384,128]{1,0:T(8,128)(2,1)} %node_ref.3, bf16[384,128]{1,0:T(8,128)(2,1)} %ncot_ref.1, ...), custom_call_target="tpu_custom_call" | custom-call | flops 10485760000 | bytes 8388608 | tf_op jit(solution)/shard_map/pallas_call | solution.py:248
  53.3 0.0 copy-done.3
  53.3 0.0 copy-start
  53.3 1.1 %copy-done = bf16[8,384,128]{2,1,0:T(8,128)(2,1)S(1)} copy-done((bf16[8,384,128]{2,1,0:T(8,128)(2,1)S(1)}, bf16[8,384,128]{2,1,0:T(8,128)(2,1)}, u32[]{:S(2)}) %copy-start) | copy-done | bytes 786456
  54.4 0.0 copy-start.1
  54.4 1.0 %copy-done.1 = f32[1024,128]{1,0:T(8,128)S(1)} copy-done((f32[1024,128]{1,0:T(8,128)S(1)}, f32[1024,128]{1,0:T(8,128)}, u32[]{:S(2)}) %copy-start.1) | copy-done | bytes 524312
  55.5 0.9 %copy-done.2 = f32[384,128]{1,0:T(8,128)S(1)} copy-done((f32[384,128]{1,0:T(8,128)S(1)}, f32[384,128]{1,0:T(8,128)}, u32[]{:S(2)}) %copy-start.2) | copy-done | bytes 196632
  56.4 0.8 copy-done.5
  57.2 24.9 %shard_map.218 = (f32[384,128]{1,0:T(8,128)S(1)}, f32[384,128]{1,0:T(8,128)S(1)}, f32[128,128]{1,0:T(8,128)S(1)}, f32[256,128]{1,0:T(8,128)S(1)}, f32[128,128]{1,0:T(8,128)S(1)}, /*index=5*/f32[6,128]{1,0:T(8,128)S(1)}) custom-call(bf16[8,384,128]{2,1,0:T(8,128)(2,1)S(1)} %copy-done, bf16[2,64,128]{2,1,0:T(8,128)(2,1)S(1)} %bitcast.11, ...), custom_call_target="tpu_custom_call" | custom-call | tf_op jit(solution)/shard_map/pallas_call | solution.py:575
  82.1 0.7 copy.31
  82.8 0.7 copy.32
  83.4 0.6 copy.33
  84.1 0.7 copy.34
  84.7 0.6 copy.35
  85.3 0.6 copy.36
  (2 shorter events, 0.0 us)
Async XLA Ops:
  2.0 0.9 %copy-start.4 = (bf16[384,128]{1,0:T(8,128)(2,1)S(1)}, bf16[384,128]{1,0:T(8,128)(2,1)}, u32[]{:S(2)}) copy-start(bf16[384,128]{1,0:T(8,128)(2,1)} %node_ref.3) | copy-start | bytes 294916
  21.2 0.9 %copy-start.6 = (bf16[8,384,128]{2,1,0:T(8,128)(2,1)}, bf16[8,384,128]{2,1,0:T(8,128)(2,1)S(1)}, u32[]{:S(2)}) copy-start(bf16[8,384,128]{2,1,0:T(8,128)(2,1)S(1)} %get-tuple-element.20.part_ref) | copy-start | bytes 2359300
  22.1 0.6 copy-start.7
  22.7 30.6 %copy-start.3 = (bf16[384,128]{1,0:T(8,128)(2,1)S(1)}, bf16[384,128]{1,0:T(8,128)(2,1)}, u32[]{:S(2)}) copy-start(bf16[384,128]{1,0:T(8,128)(2,1)} %w1_ref.1) | copy-start | bytes 294916
  53.3 1.1 %copy-start = (bf16[8,384,128]{2,1,0:T(8,128)(2,1)S(1)}, bf16[8,384,128]{2,1,0:T(8,128)(2,1)}, u32[]{:S(2)}) copy-start(bf16[8,384,128]{2,1,0:T(8,128)(2,1)} %get-tuple-element.22.sums_ref) | copy-start | bytes 2359300
  54.4 1.0 %copy-start.1 = (f32[1024,128]{1,0:T(8,128)S(1)}, f32[1024,128]{1,0:T(8,128)}, u32[]{:S(2)}) copy-start(f32[1024,128]{1,0:T(8,128)} %get-tuple-element.24) | copy-start | bytes 1572868
  55.5 0.9 %copy-start.2 = (f32[384,128]{1,0:T(8,128)S(1)}, f32[384,128]{1,0:T(8,128)}, u32[]{:S(2)}) copy-start(f32[384,128]{1,0:T(8,128)} %get-tuple-element.25.base_ref) | copy-start | bytes 589828
  56.4 0.8 copy-start.5
